TPU v7x, 128 devices: a whole 4x4x4 slice. The times are simulated.
128 devices in a mesh: dp: 4 (over y), item: 32 (over z, x, core).
Axes of the slice: x: 4, y: 4, z: 4, core: 2. Of those that a mesh axis runs over, the one named last changes fastest.
Arguments:
- queries: bfloat16 [131072, 256], P(('dp', 'item')), may hold values from -0.5 to 0.5
- item_table: float32 [131072, 256], P('item'), may hold values from -0.5 to 0.5
- adagrad_state: float32 [131072], P('item'), may hold values from 1 to 1000
- pos_owner: int32 [131072, 1], P(('dp', 'item')), may hold values from 0 to 31; in each aligned block of 1024 rows (0 to 1023, 1024 to 2047, ...) at most 96 rows name the same one
- pos_row: int32 [131072], P(('dp', 'item')), may hold values from 0 to 4095
- neg_rows: int32 [6144], P(('dp', 'item')), may hold values from 0 to 4095
Outputs:
- query_grad: bfloat16 [131072, 256], P(('dp', 'item'))
- example_loss: float32 [131072], P(('dp', 'item'))
- new_table: float32 [131072, 256], P('item')
- new_state: float32 [131072], P('item')
Inputs may be any that keep to these rules, and one draw needn't show every extreme that they name: `pos_owner`: within the rows of one device (aligned blocks of 1024 examples) no shard is named more than 96 times; some device's block names one shard exactly 96 times.
All inputs are finite; a program needn't handle non-finite values.
Results may differ from a plain program's by a relative error of at most 0.0049.
Values may be sent and summed in bfloat16 or wider, within the bound.
A program may use at most 64 MiB of HBM per device.

v0:
```python
import math
import jax
import jax.numpy as jnp
from jax import lax
from jax.sharding import PartitionSpec as P

INV_TEMP = 20.0
LEARN_RATE = 0.05
EPSILON = 1e-06


def unit_rows(matrix):
    row_norm = jnp.sqrt(jnp.sum(matrix * matrix, axis=-1, keepdims=True) + EPSILON)
    return (matrix / row_norm, row_norm)


def on_device(queries, item_table, adagrad_state, pos_owner, pos_row, neg_rows):
    ex_count = queries.shape[0]
    rows_dev = item_table.shape[0]
    feat_width = item_table.shape[1]
    item_count = lax.axis_size("item")
    capacity = 3 * ex_count // item_count
    item_index = lax.axis_index("item")
    query_hat, query_norm = unit_rows(queries.astype(jnp.float32))
    query_send = query_hat.astype(jnp.bfloat16)
    unit_table, table_norm = unit_rows(item_table)
    table_send = unit_table.astype(jnp.bfloat16)
    owners = pos_owner[:, 0]
    onehot = (owners[:, None] == jnp.arange(item_count, dtype=jnp.int32)[None, :]).astype(jnp.int32)
    earlier = jnp.cumsum(onehot, axis=0) - onehot
    slots = jnp.sum(earlier * onehot, axis=1)
    places = owners * capacity + slots
    requests = jnp.zeros((item_count * capacity,), jnp.int32).at[places].set(pos_row)
    requests = requests.reshape(item_count, capacity)
    asked_rows = lax.all_to_all(requests, "item", split_axis=0, concat_axis=0, tiled=True)
    found = table_send[asked_rows]
    returned = lax.all_to_all(found, "item", split_axis=0, concat_axis=0, tiled=True)
    pos_e = returned.reshape(item_count * capacity, feat_width)[places]
    pos_gid = owners * rows_dev + pos_row
    my_gid = item_index * rows_dev + neg_rows
    my_neg = table_send[neg_rows]
    block_rows, block_ids = (
        lax.all_gather(my_neg, "item", axis=0, tiled=True),
        lax.all_gather(my_gid, "item", axis=0, tiled=True),
    )
    all_rows, all_ids = (
        lax.all_gather(block_rows, "dp", axis=0, tiled=True),
        lax.all_gather(block_ids, "dp", axis=0, tiled=True),
    )
    negs = all_rows.shape[0]
    block_size = math.gcd(negs, 1024)
    block_count = negs // block_size
    row_blocks = all_rows.reshape(block_count, block_size, feat_width)
    id_blocks = all_ids.reshape(block_count, block_size)

    def block_scores(row_block, id_block):
        scores = (
            jnp.einsum("ed,nd->en", query_send, row_block, preferred_element_type=jnp.float32)
            * INV_TEMP
        )
        allowed = id_block[None, :] != pos_gid[:, None]
        return (scores, allowed)

    s_pos = INV_TEMP * jnp.sum(query_send.astype(jnp.float32) * pos_e.astype(jnp.float32), axis=1)

    def add_exp(carry, pieces):
        scores, allowed = block_scores(pieces[0], pieces[1])
        return (carry + jnp.sum(jnp.where(allowed, jnp.exp(scores), 0.0), axis=1), None)

    neg_totals, _ = lax.scan(add_exp, jnp.zeros((ex_count,), jnp.float32), (row_blocks, id_blocks))
    lse = jnp.log(jnp.exp(s_pos) + neg_totals)
    example_loss = lse - s_pos

    def both_products(carry, pieces):
        scores, allowed = block_scores(pieces[0], pieces[1])
        probs = jnp.where(allowed, jnp.exp(scores - lse[:, None]), 0.0).astype(jnp.bfloat16)
        carry = carry + jnp.dot(probs, pieces[0], preferred_element_type=jnp.float32)
        partial_rows = INV_TEMP * jnp.einsum(
            "en,ed->nd", probs, query_send, preferred_element_type=jnp.float32
        )
        return (carry, partial_rows)

    neg_part, partial_blocks = lax.scan(
        both_products, jnp.zeros((ex_count, feat_width), jnp.float32), (row_blocks, id_blocks)
    )
    neg_partials = partial_blocks.reshape(negs, feat_width)
    p_pos = jnp.exp(s_pos - lse)
    g_query = INV_TEMP * ((p_pos - 1.0)[:, None] * pos_e.astype(jnp.float32) + neg_part)
    query_grad = (
        (g_query - query_hat * jnp.sum(query_hat * g_query, axis=1, keepdims=True)) / query_norm
    ).astype(jnp.bfloat16)
    g_pos = INV_TEMP * (p_pos - 1.0)[:, None] * query_hat
    outbox = jnp.zeros((item_count * capacity, feat_width), jnp.float32).at[places].set(g_pos)
    outbox = outbox.reshape(item_count, capacity, feat_width)
    inbox = lax.all_to_all(
        outbox.astype(jnp.bfloat16), "item", split_axis=0, concat_axis=0, tiled=True
    ).astype(outbox.dtype)
    dense = jnp.zeros((rows_dev, feat_width), jnp.float32)
    dense = dense.at[asked_rows.reshape(-1)].add(inbox.reshape(-1, feat_width))
    neg_grad = lax.psum_scatter(neg_partials, ("dp", "item"), scatter_dimension=0, tiled=True)
    dense = dense.at[neg_rows].add(neg_grad)
    g_unit = lax.psum(dense.astype(jnp.bfloat16), "dp").astype(jnp.float32)
    g_row = (g_unit - unit_table * jnp.sum(unit_table * g_unit, axis=1, keepdims=True)) / table_norm
    new_state = adagrad_state + jnp.mean(g_row * g_row, axis=1)
    new_table = item_table - LEARN_RATE * g_row / jnp.sqrt(new_state)[:, None]
    return (query_grad, example_loss, new_table, new_state)


def solution(mesh):
    placed = (
        P(("dp", "item"), None),
        P("item", None),
        P("item"),
        P(("dp", "item"), None),
        P(("dp", "item")),
        P(("dp", "item")),
    )
    return jax.shard_map(
        on_device,
        mesh=mesh,
        in_specs=placed,
        out_specs=(P(("dp", "item"), None), P(("dp", "item")), P("item", None), P("item")),
        check_vma=False,
    )
```

profile of v0, /device:TPU:1, one launch (start us, length us, event | category | flops | bytes accessed | tf_op | source)
XLA Modules:
  0.0 490.1 jit_solution(17192636211847905702)
XLA Ops:
  7.2 3.0 multiply_reduce_fusion.1
  13.5 29.8 %all-gather = bf16[1536,256]{1,0:T(8,128)(2,1)} all-gather(bf16[48,256]{1,0:T(8,128)(2,1)S(1)} %gather_fusion.2), channel_id=2, replica_groups=mesh['dp'=4,'item'=32] {'item'}, dimensions={0}, use_global_device_ids=true | all-gather | bytes 811008 | tf_op jit(solution)/shard_map/all_gather | solution.py:43
  43.3 9.0 %reduce-window.6 = s32[32,8,128]{2,1,0:T(8,128)S(1)} reduce-window(s32[32,8,128]{2,1,0:T(8,128)S(1)} %fusion.29, s32[]{:T(128)} %constant.33.clone.1), window={size=1x1x128 pad=0_0x0_0x127_0}, to_apply=%region_2.0 | reduce-window | flops 4161536 | bytes 262148 | tf_op jit(solution)/shard_map/reduce-window
  52.8 4.3 scatter_custom_fusion
  57.2 11.8 %all_to_all.22 = s32[32,1,96]{2,1,0:T(1,128)S(1)} all-to-all(s32[32,1,96]{2,1,0:T(1,128)S(1)} %all_to_all.14), channel_id=1, replica_groups=mesh['dp'=4,'item'=32] {'item'}, dimensions={0} | all-to-all | bytes 24576 | tf_op jit(solution)/shard_map/all_to_all | solution.py:35
  69.1 13.0 %gather_fusion = bf16[3072,256]{1,0:T(8,128)(2,1)} fusion(bf16[4096,256]{1,0:T(8,128)(2,1)S(1)} %fusion.33, s32[3072]{0:T(1024)S(1)} %broadcast_clamp_fusion), kind=kCustom, calls=%fused_computation | custom fusion | bytes 3158016 | tf_op jit(solution)/shard_map/gather | solution.py:36
  82.2 4.3 all-to-all-start.1
  86.6 28.8 %all-reduce = s32[1536]{0:T(1024)S(1)} all-reduce(s32[1536]{0:T(1024)S(1)} %get-tuple-element.167), channel_id=1, replica_groups=mesh['dp'=4,'item'=32] {'item'}, use_global_device_ids=true, to_apply=%add | all-reduce | flops 1536 | bytes 12288
  115.4 9.7 %all-gather.2 = s32[4,1,1536]{2,1,0:T(1,128)S(1)} all-gather(s32[1,1,1536]{2,1,0:T(1,128)S(1)} %reshape.204), channel_id=1, replica_groups=mesh['dp'=4,'item'=32] {'dp'}, dimensions={0}, use_global_device_ids=true | all-gather | bytes 30720 | tf_op jit(solution)/shard_map/all_gather | solution.py:48
  125.5 3.9 gather_fusion.1
  129.9 12.9 %while.24 = (s32[]{:T(128)}, f32[1024]{0:T(1024)S(1)}, s32[6,1024]{1,0:T(8,128)S(1)}, s32[1024]{0:T(1024)S(1)}, bf16[6,1024,256]{2,1,0:T(8,128)(2,1)}, /*index=5*/bf16[1024,256]{1,0:T(8,128)(2,1)S(1)}, s32[]{:T(128)}, s32[]{:T(128)}) while((s32[]{:T(128)}, f32[1024]{0:T(1024)S(1)}, s32[6,1024]{1,0:T(8,128)S(1)}, ...), condition=%wide.region_9.10_spmd.clone, body=%wide.region_7.9_spmd.clone.sunk | while | flops 541066240 | bytes 1081955 | solution.py:70
  130.0 2.2 fusion.54
  132.2 2.1 fusion.54
  134.3 2.1 fusion.54
  136.4 2.1 fusion.54
  138.6 2.1 fusion.54
  140.7 2.1 fusion.54
  143.4 48.0 %while.25 = (s32[]{:T(128)}, f32[1024,256]{1,0:T(8,128)S(1)}, f32[6,1024,256]{2,1,0:T(8,128)}, s32[6,1024]{1,0:T(8,128)S(1)}, s32[1024]{0:T(1024)S(1)}, /*index=...) while((s32[]{:T(128)}, f32[1024,256]{1,0:T(8,128)S(1)}, ...), condition=%wide.region_11.12_spmd.clone, body=%wide.region_10.11_spmd.clone.sunk | while | flops 1616642048 | bytes 19945104 | solution.py:83
  143.4 2.1 fusion.61
  146.9 1.7 fusion.62
  148.6 2.8 convolution_add_fusion.2
  151.4 2.1 fusion.61
  154.9 1.8 fusion.62
  156.7 2.8 convolution_add_fusion.2
  159.5 2.1 fusion.61
  163.0 1.7 fusion.62
  164.7 2.8 convolution_add_fusion.2
  167.5 2.1 fusion.61
  171.0 1.7 fusion.62
  172.7 2.8 convolution_add_fusion.2
  175.5 2.1 fusion.61
  178.9 1.7 fusion.62
  180.6 2.8 convolution_add_fusion.2
  183.5 2.1 fusion.61
  186.9 1.7 fusion.62
  188.7 2.8 convolution_add_fusion.2
  191.5 7.1 %scatter_custom_fusion.1 = f32[3072,256]{1,0:T(8,128)} fusion(s32[1024]{0:T(1024)S(1)} %bitcast.102, f32[]{:T(128)} %constant.31.clone.1, f32[1024]{0:T(1024)S(1)} %get-tuple-element.160, bf16[1024,256]{1,0:T(8,128)(2,1)S(1)} %copy-done.3, f32[1024]{0:T(1024)S(1)} %add_sqrt_fusion.1), kind=kCustom, calls=%fused_computation.38 | custom fusion | flops 786432 | bytes 3678212 | tf_op jit(solution)/shard_map/scatter | solution.py:93
  198.6 3.2 convert_element_type.50
  201.8 10.0 %all-to-all-start.2 = ((bf16[32,96,256]{2,1,0:T(8,128)(2,1)}), bf16[32,96,256]{2,1,0:T(8,128)(2,1)S(1)}, u32[]{:S(2)}, u32[]{:S(2)}) async-start(bf16[32,96,256]{2,1,0:T(8,128)(2,1)} %bitcast.89), calls=%async_computation.2 | async-start | bytes 3145728 | tf_op jit(solution)/shard_map/all_to_all | solution.py:95
  213.2 20.9 %all-to-all-done.2 = bf16[32,96,256]{2,1,0:T(8,128)(2,1)S(1)} async-done(((bf16[32,96,256]{2,1,0:T(8,128)(2,1)}), bf16[32,96,256]{2,1,0:T(8,128)(2,1)S(1)}, u32[]{:S(2)}, u32[]{:S(2)}) %all-to-all-start.2) | async-done | bytes 1572896 | tf_op jit(solution)/shard_map/all_to_all | solution.py:95
  234.1 22.4 %scatter_custom_fusion.2 = f32[4096,256]{1,0:T(8,128)} fusion(s32[3072]{0:T(1024)S(1)} %bitcast.103, bf16[3072,256]{1,0:T(8,128)(2,1)S(1)} %bitcast.88, f32[]{:T(128)} %constant.31.clone.1), kind=kCustom, calls=%fused_computation.34 | custom fusion | flops 1572864 | bytes 5767172 | tf_op jit(solution)/shard_map/scatter-add | solution.py:99
  256.5 148.0 %reduce-scatter.2.cloned.1.call-done = f32[48,256]{1,0:T(8,128)} async-done(((f32[6144,256]{1,0:T(8,128)}), f32[48,256]{1,0:T(8,128)}) %reduce-scatter.2.cloned.1.call-update) | async-done | bytes 49168 | tf_op jit(solution)/shard_map/reduce_scatter | solution.py:100
  404.5 5.2 %scatter_fusion = f32[4096,256]{1,0:T(8,128)} fusion(f32[4096,256]{1,0:T(8,128)} %scatter_custom_fusion.2, s32[48]{0:T(128)S(1)} %get-tuple-element.166, f32[48,256]{1,0:T(8,128)} %reduce-scatter.2.cloned.1.call-done), kind=kCustom, calls=%fused_computation.6 | custom fusion | flops 12288 | bytes 147648 | tf_op jit(solution)/shard_map/scatter-add | solution.py:101
  409.8 3.8 convert_element_type.52
  415.3 56.3 %all-reduce.3.cloned.1.call-done = bf16[4096,256]{1,0:T(8,128)(2,1)} async-done(((bf16[4096,256]{1,0:T(8,128)(2,1)}), bf16[4096,256]{1,0:T(8,128)(2,1)}) %all-reduce.3.cloned.1.call-update) | async-done | bytes 2097168 | tf_op jit(solution)/shard_map/psum | solution.py:102
  471.7 3.9 fusion.13
  476.4 2.0 multiply_reduce_fusion
  479.0 4.5 divide_subtract_fusion
  (101 shorter events, 17.3 us)
Async XLA Ops:
  7.2 122.8 %all-gather.5.cloned.1.call-start = ((), (), s32[]{:S(2)}) async-start(), calls=%async_computation.6 | async-start | bytes 3932160 | tf_op jit(solution)/shard_map/all_gather | solution.py:47
  7.2 3.5 copy-start
  10.2 1.2 copy-start.11
  10.2 2.5 copy-start.10
  10.2 33.0 %copy-start.7 = (s32[1024,1]{0,1:T(1,128)S(1)}, s32[1024,1]{0,1:T(1,128)}, u32[]{:S(2)}) copy-start(s32[1024,1]{0,1:T(1,128)} %param.13) | copy-start | bytes 12292
  10.7 42.1 %copy-start.9 = (s32[1024]{0:T(1024)S(1)}, s32[1024]{0:T(1024)}, u32[]{:S(2)}) copy-start(s32[1024]{0:T(1024)} %param.14) | copy-start | bytes 12292
  69.1 56.1 %copy-start.3 = (bf16[1024,256]{1,0:T(8,128)(2,1)S(1)}, bf16[1024,256]{1,0:T(8,128)(2,1)}, u32[]{:S(2)}) copy-start(bf16[1024,256]{1,0:T(8,128)(2,1)} %param.10) | copy-start | bytes 1572868
  82.2 43.3 %all-to-all-start.1 = ((bf16[32,96,256]{2,1,0:T(8,128)(2,1)}), bf16[32,96,256]{2,1,0:T(8,128)(2,1)S(1)}, u32[]{:S(2)}, u32[]{:S(2)}) async-start(bf16[32,96,256]{2,1,0:T(8,128)(2,1)} %bitcast.90), calls=%async_computation.1 | async-start | bytes 3145728 | tf_op jit(solution)/shard_map/all_to_all | solution.py:37
  86.5 318.0 %reduce-scatter.2.cloned.1.call-start = ((), (), s32[]{:S(2)}) async-start(), calls=%async_computation.4 | async-start | bytes 6340608 | tf_op jit(solution)/shard_map/reduce_scatter | solution.py:100
  129.9 13.5 %copy-start.4 = (f32[1024,256]{1,0:T(8,128)S(1)}, f32[1024,256]{1,0:T(8,128)}, u32[]{:S(2)}) copy-start(f32[1024,256]{1,0:T(8,128)} %custom-call.1) | copy-start | bytes 3145732
  145.6 1.3 copy-start.12
  153.6 1.3 copy-start.12
  161.6 1.3 copy-start.12
  169.6 1.3 copy-start.12
  177.6 1.3 copy-start.12
  185.6 1.3 copy-start.12
  191.5 7.2 %copy-start.5 = (f32[1024,256]{1,0:T(8,128)}, f32[1024,256]{1,0:T(8,128)S(1)}, u32[]{:S(2)}) copy-start(f32[1024,256]{1,0:T(8,128)S(1)} %get-tuple-element.80) | copy-start | bytes 3145732
  201.8 32.3 %all-to-all-start.2 = ((bf16[32,96,256]{2,1,0:T(8,128)(2,1)}), bf16[32,96,256]{2,1,0:T(8,128)(2,1)S(1)}, u32[]{:S(2)}, u32[]{:S(2)}) async-start(bf16[32,96,256]{2,1,0:T(8,128)(2,1)} %bitcast.89), calls=%async_computation.2 | async-start | bytes 3145728 | tf_op jit(solution)/shard_map/all_to_all | solution.py:95
  211.8 259.9 %all-reduce.3.cloned.1.call-start = ((), (), s32[]{:S(2)}) async-start(), calls=%async_computation.5 | async-start | bytes 4194304 | tf_op jit(solution)/shard_map/psum | solution.py:102
  409.8 3.8 copy-start.6
  471.7 4.1 copy-start.1
  471.7 4.7 copy-start.2
  476.4 2.0 copy-start.8
Sparse Core Ops, SparseCore 0:
  43.4 38.4 all-gather.4
  191.6 212.8 reduce-scatter.1
  413.7 57.9 all-reduce.2
where the time goes:
time: 491 us; the launch traced here: 490 us
  waiting for transfers between devices  225 us (46%)
  blocking collectives  80.1 us (16%)
  other arithmetic  69.7 us (14%)
  matrix products  52.4 us (11%)
  local copies, waits for them, and re-layouts  32.9 us (7%)
  between operations  14.8 us (3%)
  starting transfers between devices  14.4 us (3%)
    reduce_scatter x1, waiting for transfers between devices, on_device(): lax.psum_scatter(neg_partials, ('dp', 'item'), scatter_dimension=0, tiled...  148 us
    psum x1, waiting for transfers between devices, on_device(): g_unit = lax.psum(dense.astype(jnp.bfloat16), 'dp').astype(jnp.float32)  56.3 us
    all_gather x1, blocking collectives, on_device(): lax.all_gather(my_neg, 'item', axis=0, tiled=True)  29.8 us
    unnamed x1, blocking collectives  28.8 us
    dot_general x12, matrix products, block_scores(): jnp.einsum('ed,nd->en', query_send, row_block, preferred_element_type=jnp...  25.4 us
    scatter-add x1, other arithmetic, on_device(): dense = dense.at[asked_rows.reshape(-1)].add(inbox.reshape(-1, feat_width))  22.4 us
    all_to_all x1, waiting for transfers between devices, on_device(): lax.all_to_all(outbox.astype(jnp.bfloat16), 'item', split_axis=0, concat_...  20.9 us
    dot_general x6, matrix products, both_products(): jnp.dot(probs, pieces[0], preferred_element_type=jnp.float32)  16.7 us
  transfers between devices with their start and end apart: 5, of which 3 were waited for; matrix products, arithmetic and copies ran while one was open for 14% of the time, Pallas kernels for 0%

commit v1 on v0

--- a/solution.py
+++ b/solution.py
@@ -7,6 +7,12 @@
 INV_TEMP = 20.0
 LEARN_RATE = 0.05
 EPSILON = 1e-06
+
+
+def summed_here(shard, mesh_axis):
+    parts = lax.all_gather(shard, mesh_axis, axis=0, tiled=False)
+    total = parts.sum(axis=0)
+    return total
 
 
 def unit_rows(matrix):
@@ -99,7 +105,7 @@
     dense = dense.at[asked_rows.reshape(-1)].add(inbox.reshape(-1, feat_width))
     neg_grad = lax.psum_scatter(neg_partials, ("dp", "item"), scatter_dimension=0, tiled=True)
     dense = dense.at[neg_rows].add(neg_grad)
-    g_unit = lax.psum(dense.astype(jnp.bfloat16), "dp").astype(jnp.float32)
+    g_unit = summed_here(dense.astype(jnp.bfloat16), "dp").astype(jnp.float32)
     g_row = (g_unit - unit_table * jnp.sum(unit_table * g_unit, axis=1, keepdims=True)) / table_norm
     new_state = adagrad_state + jnp.mean(g_row * g_row, axis=1)
     new_table = item_table - LEARN_RATE * g_row / jnp.sqrt(new_state)[:, None]

time: 491 us -> 521 us (1.061)
  waiting for transfers between devices: 225 us -> 250 us
  other arithmetic: 69.7 us -> 75.1 us
    all_gather x0 -> x1, waiting for transfers between devices: none -> 80.7 us  [summed_here(): parts = lax.all_gather(shard, mesh_axis, axis=0, tiled=False)]
    psum x1 -> x0, waiting for transfers between devices: 56.3 us -> none  [on_device(): g_unit = lax.psum(dense.astype(jnp.bfloat16), 'dp').astype(jnp.float32)]
    reduce_sum x0 -> x1, other arithmetic: none -> 6.04 us  [summed_here(): total = parts.sum(axis=0)]
  transfers between devices with their start and end apart: 5 -> 5, of which waited for: 3 -> 3; matrix products, arithmetic and copies ran while one was open for 14% -> 13% of each run, Pallas kernels for 0% -> 0%
where the time goes in v1:
time: 521 us; the launch traced here: 519 us
  waiting for transfers between devices  250 us (48%)
  blocking collectives  80.1 us (15%)
  other arithmetic  75.1 us (14%)
  matrix products  52.4 us (10%)
  local copies, waits for them, and re-layouts  32.4 us (6%)
  between operations  14.8 us (3%)
  starting transfers between devices  14.4 us (3%)
    reduce_scatter x1, waiting for transfers between devices, on_device(): lax.psum_scatter(neg_partials, ('dp', 'item'), scatter_dimension=0, tiled...  148 us
    all_gather x1, waiting for transfers between devices, summed_here(): parts = lax.all_gather(shard, mesh_axis, axis=0, tiled=False)  80.7 us
    all_gather x1, blocking collectives, on_device(): lax.all_gather(my_neg, 'item', axis=0, tiled=True)  29.8 us
    unnamed x1, blocking collectives  28.8 us
    dot_general x12, matrix products, block_scores(): jnp.einsum('ed,nd->en', query_send, row_block, preferred_element_type=jnp...  25.4 us
    scatter-add x1, other arithmetic, on_device(): dense = dense.at[asked_rows.reshape(-1)].add(inbox.reshape(-1, feat_width))  22.4 us
    all_to_all x1, waiting for transfers between devices, on_device(): lax.all_to_all(outbox.astype(jnp.bfloat16), 'item', split_axis=0, concat_...  20.9 us
    dot_general x6, matrix products, both_products(): jnp.dot(probs, pieces[0], preferred_element_type=jnp.float32)  16.7 us
  transfers between devices with their start and end apart: 5, of which 3 were waited for; matrix products, arithmetic and copies ran while one was open for 13% of the time, Pallas kernels for 0%

profile of v1, /device:TPU:1, one launch (start us, length us, event | category | flops | bytes accessed | tf_op | source)
XLA Modules:
  0.0 519.4 jit_solution(15889200706058071809)
XLA Ops:
  7.2 3.0 multiply_reduce_fusion.1
  13.5 29.8 %all-gather = bf16[1536,256]{1,0:T(8,128)(2,1)} all-gather(bf16[48,256]{1,0:T(8,128)(2,1)S(1)} %gather_fusion.2), channel_id=2, replica_groups=mesh['dp'=4,'item'=32] {'item'}, dimensions={0}, use_global_device_ids=true | all-gather | bytes 811008 | tf_op jit(solution)/shard_map/all_gather | solution.py:49
  43.3 9.0 %reduce-window.6 = s32[32,8,128]{2,1,0:T(8,128)S(1)} reduce-window(s32[32,8,128]{2,1,0:T(8,128)S(1)} %fusion.29, s32[]{:T(128)} %constant.16.clone.1), window={size=1x1x128 pad=0_0x0_0x127_0}, to_apply=%region_2.0 | reduce-window | flops 4161536 | bytes 262148 | tf_op jit(solution)/shard_map/reduce-window
  52.8 4.3 scatter_custom_fusion
  57.2 11.8 %all_to_all.22 = s32[32,1,96]{2,1,0:T(1,128)S(1)} all-to-all(s32[32,1,96]{2,1,0:T(1,128)S(1)} %all_to_all.14), channel_id=1, replica_groups=mesh['dp'=4,'item'=32] {'item'}, dimensions={0} | all-to-all | bytes 24576 | tf_op jit(solution)/shard_map/all_to_all | solution.py:41
  69.1 13.0 %gather_fusion = bf16[3072,256]{1,0:T(8,128)(2,1)} fusion(bf16[4096,256]{1,0:T(8,128)(2,1)S(1)} %fusion.33, s32[3072]{0:T(1024)S(1)} %broadcast_clamp_fusion), kind=kCustom, calls=%fused_computation | custom fusion | bytes 3158016 | tf_op jit(solution)/shard_map/gather | solution.py:42
  82.2 4.3 all-to-all-start.1
  86.6 28.8 %all-reduce = s32[1536]{0:T(1024)S(1)} all-reduce(s32[1536]{0:T(1024)S(1)} %get-tuple-element.167), channel_id=1, replica_groups=mesh['dp'=4,'item'=32] {'item'}, use_global_device_ids=true, to_apply=%add | all-reduce | flops 1536 | bytes 12288
  115.4 9.7 %all-gather.3 = s32[4,1,1536]{2,1,0:T(1,128)S(1)} all-gather(s32[1,1,1536]{2,1,0:T(1,128)S(1)} %reshape.205), channel_id=1, replica_groups=mesh['dp'=4,'item'=32] {'dp'}, dimensions={0}, use_global_device_ids=true | all-gather | bytes 30720 | tf_op jit(solution)/shard_map/all_gather | solution.py:54
  125.5 3.9 gather_fusion.1
  129.9 12.9 %while.24 = (s32[]{:T(128)}, f32[1024]{0:T(1024)S(1)}, s32[6,1024]{1,0:T(8,128)S(1)}, s32[1024]{0:T(1024)S(1)}, bf16[6,1024,256]{2,1,0:T(8,128)(2,1)}, /*index=5*/bf16[1024,256]{1,0:T(8,128)(2,1)S(1)}, s32[]{:T(128)}, s32[]{:T(128)}) while((s32[]{:T(128)}, f32[1024]{0:T(1024)S(1)}, s32[6,1024]{1,0:T(8,128)S(1)}, ...), condition=%wide.region_9.10_spmd.clone, body=%wide.region_7.9_spmd.clone.sunk | while | flops 541066240 | bytes 1081955 | solution.py:76
  130.0 2.2 fusion.54
  132.2 2.1 fusion.54
  134.3 2.1 fusion.54
  136.4 2.1 fusion.54
  138.6 2.1 fusion.54
  140.7 2.1 fusion.54
  143.4 48.0 %while.25 = (s32[]{:T(128)}, f32[1024,256]{1,0:T(8,128)S(1)}, f32[6,1024,256]{2,1,0:T(8,128)}, s32[6,1024]{1,0:T(8,128)S(1)}, s32[1024]{0:T(1024)S(1)}, /*index=...) while((s32[]{:T(128)}, f32[1024,256]{1,0:T(8,128)S(1)}, ...), condition=%wide.region_11.12_spmd.clone, body=%wide.region_10.11_spmd.clone.sunk | while | flops 1616642048 | bytes 19945104 | solution.py:89
  143.4 2.1 fusion.61
  146.9 1.7 fusion.62
  148.6 2.8 convolution_add_fusion.2
  151.4 2.1 fusion.61
  154.9 1.8 fusion.62
  156.7 2.8 convolution_add_fusion.2
  159.5 2.1 fusion.61
  163.0 1.7 fusion.62
  164.7 2.8 convolution_add_fusion.2
  167.5 2.1 fusion.61
  171.0 1.7 fusion.62
  172.7 2.8 convolution_add_fusion.2
  175.5 2.1 fusion.61
  180.6 2.8 convolution_add_fusion.2
  183.5 2.1 fusion.61
  186.9 1.7 fusion.62
  188.7 2.8 convolution_add_fusion.2
  191.5 7.1 %scatter_custom_fusion.1 = f32[3072,256]{1,0:T(8,128)} fusion(s32[1024]{0:T(1024)S(1)} %bitcast.104, f32[]{:T(128)} %constant.32.clone.1, f32[1024]{0:T(1024)S(1)} %get-tuple-element.160, bf16[1024,256]{1,0:T(8,128)(2,1)S(1)} %copy-done.2, f32[1024]{0:T(1024)S(1)} %add_sqrt_fusion.1), kind=kCustom, calls=%fused_computation.38 | custom fusion | flops 786432 | bytes 3678212 | tf_op jit(solution)/shard_map/scatter | solution.py:99
  198.6 3.2 convert_element_type.52
  201.8 10.0 %all-to-all-start.2 = ((bf16[32,96,256]{2,1,0:T(8,128)(2,1)}), bf16[32,96,256]{2,1,0:T(8,128)(2,1)S(1)}, u32[]{:S(2)}, u32[]{:S(2)}) async-start(bf16[32,96,256]{2,1,0:T(8,128)(2,1)} %bitcast.91), calls=%async_computation.2 | async-start | bytes 3145728 | tf_op jit(solution)/shard_map/all_to_all | solution.py:101
  213.2 20.9 %all-to-all-done.2 = bf16[32,96,256]{2,1,0:T(8,128)(2,1)S(1)} async-done(((bf16[32,96,256]{2,1,0:T(8,128)(2,1)}), bf16[32,96,256]{2,1,0:T(8,128)(2,1)S(1)}, u32[]{:S(2)}, u32[]{:S(2)}) %all-to-all-start.2) | async-done | bytes 1572896 | tf_op jit(solution)/shard_map/all_to_all | solution.py:101
  234.1 22.4 %scatter_custom_fusion.2 = f32[4096,256]{1,0:T(8,128)} fusion(s32[3072]{0:T(1024)S(1)} %bitcast.105, bf16[3072,256]{1,0:T(8,128)(2,1)S(1)} %bitcast.90, f32[]{:T(128)} %constant.32.clone.1), kind=kCustom, calls=%fused_computation.34 | custom fusion | flops 1572864 | bytes 5767172 | tf_op jit(solution)/shard_map/scatter-add | solution.py:105
  256.5 148.0 %reduce-scatter.2.cloned.1.call-done = f32[48,256]{1,0:T(8,128)} async-done(((f32[6144,256]{1,0:T(8,128)}), f32[48,256]{1,0:T(8,128)}) %reduce-scatter.2.cloned.1.call-update) | async-done | bytes 49168 | tf_op jit(solution)/shard_map/reduce_scatter | solution.py:106
  404.5 5.2 %scatter_fusion = f32[4096,256]{1,0:T(8,128)} fusion(f32[4096,256]{1,0:T(8,128)} %scatter_custom_fusion.2, s32[48]{0:T(128)S(1)} %get-tuple-element.166, f32[48,256]{1,0:T(8,128)} %reduce-scatter.2.cloned.1.call-done), kind=kCustom, calls=%fused_computation.6 | custom fusion | flops 12288 | bytes 147648 | tf_op jit(solution)/shard_map/scatter-add | solution.py:107
  409.8 3.9 convert_element_type.54
  415.4 80.7 %all-gather.9.cloned.1.call-done = bf16[16384,256]{1,0:T(8,128)(2,1)} async-done(((bf16[4096,256]{1,0:T(8,128)(2,1)}), bf16[16384,256]{1,0:T(8,128)(2,1)}) %all-gather.9.cloned.1.call-update) | async-done | bytes 8388624 | tf_op jit(solution)/shard_map/all_gather | solution.py:13
  496.2 6.0 %reduce_sum.92 = bf16[4096,256]{1,0:T(8,128)(2,1)S(1)} reduce(bf16[4,4096,256]{2,1,0:T(8,128)(2,1)} %bitcast.89, bf16[]{:T(256)} %constant.22.clone.1), dimensions={0}, to_apply=%region_17.18 | reduce | flops 3145728 | bytes 10485762 | tf_op jit(solution)/shard_map/reduce_sum | solution.py:14
  502.2 3.2 fusion.13
  505.7 2.0 multiply_reduce_fusion
  508.3 4.6 divide_subtract_fusion
  (100 shorter events, 18.5 us)
Async XLA Ops:
  7.2 122.8 %all-gather.7.cloned.1.call-start = ((), (), s32[]{:S(2)}) async-start(), calls=%async_computation.5 | async-start | bytes 3932160 | tf_op jit(solution)/shard_map/all_gather | solution.py:53
  7.2 3.5 copy-start
  10.2 1.2 copy-start.10
  10.2 2.5 copy-start.9
  10.2 33.0 %copy-start.6 = (s32[1024,1]{0,1:T(1,128)S(1)}, s32[1024,1]{0,1:T(1,128)}, u32[]{:S(2)}) copy-start(s32[1024,1]{0,1:T(1,128)} %param.13) | copy-start | bytes 12292
  10.7 42.1 %copy-start.8 = (s32[1024]{0:T(1024)S(1)}, s32[1024]{0:T(1024)}, u32[]{:S(2)}) copy-start(s32[1024]{0:T(1024)} %param.14) | copy-start | bytes 12292
  69.1 56.1 %copy-start.2 = (bf16[1024,256]{1,0:T(8,128)(2,1)S(1)}, bf16[1024,256]{1,0:T(8,128)(2,1)}, u32[]{:S(2)}) copy-start(bf16[1024,256]{1,0:T(8,128)(2,1)} %param.10) | copy-start | bytes 1572868
  82.2 43.3 %all-to-all-start.1 = ((bf16[32,96,256]{2,1,0:T(8,128)(2,1)}), bf16[32,96,256]{2,1,0:T(8,128)(2,1)S(1)}, u32[]{:S(2)}, u32[]{:S(2)}) async-start(bf16[32,96,256]{2,1,0:T(8,128)(2,1)} %bitcast.92), calls=%async_computation.1 | async-start | bytes 3145728 | tf_op jit(solution)/shard_map/all_to_all | solution.py:43
  86.5 318.0 %reduce-scatter.2.cloned.1.call-start = ((), (), s32[]{:S(2)}) async-start(), calls=%async_computation.4 | async-start | bytes 6340608 | tf_op jit(solution)/shard_map/reduce_scatter | solution.py:106
  129.9 13.5 %copy-start.3 = (f32[1024,256]{1,0:T(8,128)S(1)}, f32[1024,256]{1,0:T(8,128)}, u32[]{:S(2)}) copy-start(f32[1024,256]{1,0:T(8,128)} %custom-call.1) | copy-start | bytes 3145732
  145.6 1.3 copy-start.11
  153.6 1.3 copy-start.11
  161.6 1.3 copy-start.11
  169.6 1.3 copy-start.11
  177.6 1.3 copy-start.11
  185.6 1.3 copy-start.11
  191.5 7.2 %copy-start.4 = (f32[1024,256]{1,0:T(8,128)}, f32[1024,256]{1,0:T(8,128)S(1)}, u32[]{:S(2)}) copy-start(f32[1024,256]{1,0:T(8,128)S(1)} %get-tuple-element.80) | copy-start | bytes 3145732
  201.8 32.3 %all-to-all-start.2 = ((bf16[32,96,256]{2,1,0:T(8,128)(2,1)}), bf16[32,96,256]{2,1,0:T(8,128)(2,1)S(1)}, u32[]{:S(2)}, u32[]{:S(2)}) async-start(bf16[32,96,256]{2,1,0:T(8,128)(2,1)} %bitcast.91), calls=%async_computation.2 | async-start | bytes 3145728 | tf_op jit(solution)/shard_map/all_to_all | solution.py:101
  211.8 284.4 %all-gather.9.cloned.1.call-start = ((), (), s32[]{:S(2)}) async-start(), calls=%async_computation.6 | async-start | bytes 10485760 | tf_op jit(solution)/shard_map/all_gather | solution.py:13
  409.8 3.9 copy-start.5
  502.2 3.5 copy-start.1
  505.7 2.0 copy-start.7
Sparse Core Ops, SparseCore 0:
  43.4 38.4 all-gather.6
  191.6 212.8 reduce-scatter.1
  413.8 82.3 all-gather.8
